TPU v7x, 32 devices: a whole 2x2x4 slice. The times are simulated.
32 devices in a mesh: parts: 2 (over x), slab: 16 (over z, y, core).
Axes of the slice: x: 2, y: 2, z: 4, core: 2. Of those that a mesh axis runs over, the one named last changes fastest.
Arguments:
- volume: bfloat16 [32, 16, 64, 256], P(('parts', 'slab')), parts along dimension 0, may hold values from -6 to 6
- plane_weight: bfloat16 [2, 5, 5, 16, 256], replicated, may hold values from -0.3125 to 0.3125
- norm_gain: bfloat16 [2, 256], replicated, may hold values from 0.099609375 to 1.8984375
- expand_weight: bfloat16 [2, 256, 1024], replicated, may hold values from -0.375 to 0.375
- down_weight: bfloat16 [2, 1024, 256], replicated, may hold values from -0.1875 to 0.1875
- depth_weight: bfloat16 [2, 3, 256], replicated, may hold values from -3 to 3
Outputs:
- features: bfloat16 [32, 16, 64, 256], P(('parts', 'slab')), parts along dimension 0
There are 2 independent parts, one for each index of `parts`. A program takes and returns all parts, laid end to end along the dimension named above; an argument that names none is the same for every part. Nothing has to cross between parts.
All inputs are finite; a program needn't handle non-finite values.
Results may differ from a plain program's by a relative error of at most 0.01.
Values may be sent and summed in bfloat16 or wider, within the bound.
A program may use at most 64 MiB of HBM per device.

v0:
```python
import jax
import jax.numpy as jnp
from jax import lax
from jax.sharding import PartitionSpec as P

FIRST_DILATION = 1
SECOND_DILATION = 4


epsilon = 1e-06


def shifted(block, axis, distance):
    devices = range(lax.axis_size(axis))
    route = [(i - distance, i) for i in devices if i - distance in devices]
    return lax.ppermute(block, axis, route)


def dense_taps(weight):
    group_size = weight.shape[2]
    channels = weight.shape[3]
    block_size = min(channels, 128)
    block_count = channels // block_size
    row_group = jnp.arange(channels)[:, None] // group_size
    column_cluster = jnp.arange(channels)[None, :] // group_size
    tiled_taps = jnp.tile(weight, (1, 1, channels // group_size, 1))
    masked = jnp.where(row_group == column_cluster, tiled_taps, jnp.zeros_like(tiled_taps))
    blocks = jnp.stack(
        [
            masked[
                :,
                :,
                index_b * block_size : (index_b + 1) * block_size,
                index_b * block_size : (index_b + 1) * block_size,
            ]
            for index_b in range(block_count)
        ],
        axis=2,
    )
    return blocks.transpose(0, 2, 1, 3, 4).reshape(5, block_count, 5 * block_size, block_size)


def plane_conv(current, kernel_taps):
    slab_depth, extent_x, extent_y, channels = current.shape
    block_count = kernel_taps.shape[1]
    block_size = channels // block_count
    padded = jnp.pad(current, ((0, 0), (2, 2), (2, 2), (0, 0)))
    accumulated = jnp.zeros((slab_depth, extent_x, extent_y, block_count, block_size), jnp.float32)
    for offset_row in range(5):
        pieces = [
            padded[
                :, offset_row : offset_row + extent_x, offset_col : offset_col + extent_y
            ].reshape(slab_depth, extent_x, extent_y, block_count, block_size)
            for offset_col in range(5)
        ]
        window = jnp.concatenate(pieces, axis=-1)
        accumulated = accumulated + jnp.einsum(
            "zxybk,bkj->zxybj", window, kernel_taps[offset_row], preferred_element_type=jnp.float32
        )
    return accumulated.reshape(slab_depth, extent_x, extent_y, channels)


def shards(volume, plane_weight, norm_gain, expand_weight, down_weight, depth_weight):
    current = volume
    slab_depth, extent_x, extent_y, channels = current.shape
    for layer_number, dilation_factor in enumerate((FIRST_DILATION, SECOND_DILATION)):
        kernel_taps = dense_taps(plane_weight[layer_number])
        conv_out = plane_conv(current, kernel_taps)
        scale_inv = lax.rsqrt(jnp.mean(conv_out * conv_out, axis=-1, keepdims=True) + epsilon)
        normed = (conv_out * scale_inv * norm_gain[layer_number].astype(jnp.float32)).astype(
            jnp.bfloat16
        )
        flat_rows = normed.reshape(-1, channels)
        hidden = jax.nn.silu(
            jnp.dot(flat_rows, expand_weight[layer_number], preferred_element_type=jnp.float32)
        ).astype(jnp.bfloat16)
        mixed = jnp.dot(
            hidden, down_weight[layer_number], preferred_element_type=jnp.float32
        ).astype(jnp.bfloat16)
        mixed = mixed.reshape(slab_depth, extent_x * extent_y, channels)
        coeffs = depth_weight[layer_number].astype(jnp.float32)
        reach = dilation_factor // slab_depth
        from_lower = shifted(mixed, "slab", reach)
        from_upper = shifted(mixed, "slab", -reach)
        depth_term = (
            coeffs[0] * from_lower.astype(jnp.float32)
            + coeffs[1] * mixed.astype(jnp.float32)
            + coeffs[2] * from_upper.astype(jnp.float32)
        )
        returned = depth_term.astype(jnp.bfloat16)
        current = (
            current.astype(jnp.float32) + returned.reshape(current.shape).astype(jnp.float32)
        ).astype(jnp.bfloat16)
    return current


def solution(mesh):
    placed = (P(("parts", "slab"), None, None, None), P(), P(), P(), P(), P())
    return jax.shard_map(
        shards,
        mesh=mesh,
        in_specs=placed,
        out_specs=P(("parts", "slab"), None, None, None),
        check_vma=False,
    )
```

profile of v0, /device:TPU:1, one launch (start us, length us, event | category | flops | bytes accessed | tf_op | source)
XLA Modules:
  0.0 79.0 jit_solution(9369417095266496980)
XLA Ops:
  0.0 8.3 %fusion.31 = (bf16[1,16,8,2,8,128]{5,4,3,2,1,0:T(8,128)(2,1)S(1)}, bf16[1,16,8,2,8,128]{5,4,3,2,1,0:T(8,128)(2,1)S(1)}, bf16[1,16,8,2,8,128]{5,4,3,2,1,0:T(8,128...) fusion(bf16[1,16,64,256]{3,2,1,0:T(8,128)(2,1)} %param.6), kind=kLoop, calls=%fused_computation.97 | loop fusion | bytes 10485760
  10.2 2.1 %bitcast_select_fusion = (bf16[5,5,256,256]{3,2,1,0:T(8,128)(2,1)}, bf16[5,5,256,256]{3,2,1,0:T(8,128)(2,1)S(1)}) fusion(pred[256,256]{1,0:T(8,128)(4,1)S(1)} %broadcast_compare_fusion, bf16[5,5,16,256]{3,2,1,0:T(8,128)(2,1)S(1)} %get-tuple-element.71, bf16[5,5,16,256]{3,2,1,0:T(8,128)(2,1)S(1)} %get-tuple-element.72), kind=kLoop, calls=%fused_computation.2 | loop fusion | flops 3276800 | bytes 7028736 | tf_op jit(solution)/shard_map/jit(_where)/select_n | solution.py:27
  14.8 0.8 %fusion.97 = f32[2,128,1024]{1,2,0:S(1)} fusion(bf16[2,640,1024]{1,2,0:T(8,128)(2,1)S(1)} %bitcast.405, bf16[2,640,128]{2,1,0:T(8,128)(2,1)S(1)} %bitcast.423), kind=kOutput, calls=%fused_computation.218 | convolution fusion | flops 335544320 | bytes 3997696
  15.6 0.8 %fusion.98 = f32[2,128,1024]{1,2,0:S(1)} fusion(bf16[2,640,1024]{1,2,0:T(8,128)(2,1)S(1)} %bitcast.410, bf16[2,640,128]{2,1,0:T(8,128)(2,1)S(1)} %bitcast.422), kind=kOutput, calls=%fused_computation.219 | convolution fusion | flops 335544320 | bytes 3997696
  18.4 0.8 %fusion.100 = f32[2,128,1024]{1,2,0:S(1)} fusion(bf16[2,640,1024]{1,2,0:T(8,128)(2,1)S(1)} %bitcast.409, bf16[2,640,128]{2,1,0:T(8,128)(2,1)S(1)} %bitcast.421), kind=kOutput, calls=%fused_computation.221 | convolution fusion | flops 335544320 | bytes 3997696
  19.2 0.8 %fusion.99 = f32[2,128,1024]{1,2,0:S(1)} fusion(bf16[2,640,1024]{1,2,0:T(8,128)(2,1)S(1)} %bitcast.406, bf16[2,640,128]{2,1,0:T(8,128)(2,1)S(1)} %bitcast.420), kind=kOutput, calls=%fused_computation.220 | convolution fusion | flops 335544320 | bytes 3997696
  21.0 0.8 %fusion.96 = f32[2,128,1024]{1,2,0:S(1)} fusion(bf16[2,640,1024]{1,2,0:T(8,128)(2,1)S(1)} %bitcast.402, bf16[2,640,128]{2,1,0:T(8,128)(2,1)S(1)} %bitcast.418), kind=kOutput, calls=%fused_computation.217 | convolution fusion | flops 335544320 | bytes 3997696
  23.5 2.6 %fusion.7 = bf16[1024,256]{1,0:T(8,128)(2,1)S(1)} fusion(bf16[128,8,2,128]{3,2,1,0:T(2,128)(2,1)S(1)} %bitcast.428, bf16[2,1024,256]{2,1,0:T(8,128)(2,1)S(1)} %copy-done.4, bf16[2,256,1024]{2,1,0:T(8,128)(2,1)} %param.9), kind=kOutput, calls=%fused_computation.11 | convolution fusion | flops 1079246848 | bytes 2097152 | tf_op jit(solution)/shard_map/dot_general | solution.py:77
  26.1 4.5 %collective-permute-start = (bf16[1,1024,256]{2,1,0:T(8,128)(2,1)S(1)}, bf16[1,1024,256]{2,1,0:T(8,128)(2,1)S(1)}, u32[]{:S(2)}, u32[]{:S(2)}) collective-permute-start(bf16[1,1024,256]{2,1,0:T(8,128)(2,1)S(1)} %bitcast.424), channel_id=1, source_target_pairs={{0,1},{1,2},{2,3},{3,4},{4,5},{5,6},{6,7},{7,8},{8,9},{9,10},{10,1... | collective-permute-start | bytes 1572872 | tf_op jit(solution)/shard_map/ppermute | solution.py:16
  30.7 1.9 %collective-permute-start.1 = (bf16[1,1024,256]{2,1,0:T(8,128)(2,1)S(1)}, bf16[1,1024,256]{2,1,0:T(8,128)(2,1)S(1)}, u32[]{:S(2)}, u32[]{:S(2)}) collective-permute-start(bf16[1,1024,256]{2,1,0:T(8,128)(2,1)S(1)} %bitcast.425), channel_id=1, source_target_pairs={{1,0},{2,1},{3,2},{4,3},{5,4},{6,5},{7,6},{8,7},{9,8},{10,9},{11,1... | collective-permute-start | bytes 1572872 | tf_op jit(solution)/shard_map/ppermute | solution.py:16
  32.6 1.6 %slice_bitcast_fusion.1 = (bf16[5,5,1,128,128]{4,3,1,0,2:T(8,128)(2,1)S(1)}, bf16[5,5,1,128,128]{4,3,1,0,2:T(8,128)(2,1)S(1)}) fusion(bf16[5,5,256,256]{3,2,1,0:T(8,128)(2,1)} %get-tuple-element.73), kind=kLoop, calls=%fused_computation.83 | loop fusion | bytes 3276800 | tf_op jit(solution)/shard_map/stack | solution.py:28
  34.6 7.8 %collective-permute-done = bf16[1,1024,256]{2,1,0:T(8,128)(2,1)S(1)} collective-permute-done((bf16[1,1024,256]{2,1,0:T(8,128)(2,1)S(1)}, bf16[1,1024,256]{2,1,0:T(8,128)(2,1)S(1)}, u32[]{:S(2)}, u32[]{:S(2)}) %collective-permute-start) | collective-permute-done | bytes 524320 | tf_op jit(solution)/shard_map/ppermute | solution.py:16
  42.9 3.0 %fusion.55 = (bf16[1,16,8,2,8,128]{5,4,3,2,1,0:T(8,128)(2,1)S(1)}, bf16[1,16,8,2,8,128]{5,4,3,2,1,0:T(8,128)(2,1)S(1)}, bf16[1,16,8,2,8,128]{5,4,3,2,1,0:T(8,128...) fusion(bf16[1,16,64,256]{3,2,1,0:T(8,128)(2,1)S(1)} %fusion.9), kind=kLoop, calls=%fused_computation.121 | loop fusion | bytes 10485760
  48.6 0.8 %fusion.102 = f32[2,128,1024]{1,2,0:S(1)} fusion(bf16[2,640,1024]{1,2,0:T(8,128)(2,1)S(1)} %bitcast.408, bf16[2,640,128]{2,1,0:T(8,128)(2,1)S(1)} %bitcast.419), kind=kOutput, calls=%fused_computation.223 | convolution fusion | flops 335544320 | bytes 3997696
  50.4 0.8 %fusion.101 = f32[2,128,1024]{1,2,0:S(1)} fusion(bf16[2,640,1024]{1,2,0:T(8,128)(2,1)S(1)} %bitcast.407, bf16[2,640,128]{2,1,0:T(8,128)(2,1)S(1)} %bitcast.417), kind=kOutput, calls=%fused_computation.222 | convolution fusion | flops 335544320 | bytes 3997696
  51.7 0.8 %fusion.103 = f32[2,128,1024]{1,2,0:S(1)} fusion(bf16[2,640,1024]{1,2,0:T(8,128)(2,1)S(1)} %bitcast.411, bf16[2,640,128]{2,1,0:T(8,128)(2,1)S(1)} %bitcast.416), kind=kOutput, calls=%fused_computation.224 | convolution fusion | flops 335544320 | bytes 3997696
  53.5 0.8 %fusion.104 = f32[2,128,1024]{1,2,0:S(1)} fusion(bf16[2,640,1024]{1,2,0:T(8,128)(2,1)S(1)} %bitcast.404, bf16[2,640,128]{2,1,0:T(8,128)(2,1)S(1)} %bitcast.415), kind=kOutput, calls=%fused_computation.225 | convolution fusion | flops 335544320 | bytes 3997696
  55.3 0.8 %fusion.105 = f32[2,128,1024]{1,2,0:S(1)} fusion(bf16[2,640,1024]{1,2,0:T(8,128)(2,1)S(1)} %bitcast.403, bf16[2,640,128]{2,1,0:T(8,128)(2,1)S(1)} %bitcast.414), kind=kOutput, calls=%fused_computation.226 | convolution fusion | flops 335544320 | bytes 3997696
  57.3 2.4 %fusion.6 = bf16[1024,256]{1,0:T(8,128)(2,1)S(1)} fusion(bf16[128,8,2,128]{3,2,1,0:T(2,128)(2,1)S(1)} %bitcast.429, bf16[2,1024,256]{2,1,0:T(8,128)(2,1)S(1)} %copy-done.4, bf16[2,256,1024]{2,1,0:T(8,128)(2,1)} %param.9), kind=kOutput, calls=%fused_computation.10 | convolution fusion | flops 1079246848 | bytes 2097152 | tf_op jit(solution)/shard_map/dot_general | solution.py:77
  59.7 4.8 %collective-permute-start.2 = (bf16[1,1024,256]{2,1,0:T(8,128)(2,1)S(1)}, bf16[1,1024,256]{2,1,0:T(8,128)(2,1)S(1)}, u32[]{:S(2)}, u32[]{:S(2)}) collective-permute-start(bf16[1,1024,256]{2,1,0:T(8,128)(2,1)S(1)} %bitcast.426), channel_id=1, source_target_pairs={{0,4},{1,5},{2,6},{3,7},{4,8},{5,9},{6,10},{7,11},{8,12},{9,13},{1... | collective-permute-start | bytes 1572872 | tf_op jit(solution)/shard_map/ppermute | solution.py:16
  64.5 1.3 %collective-permute-start.3 = (bf16[1,1024,256]{2,1,0:T(8,128)(2,1)S(1)}, bf16[1,1024,256]{2,1,0:T(8,128)(2,1)S(1)}, u32[]{:S(2)}, u32[]{:S(2)}) collective-permute-start(bf16[1,1024,256]{2,1,0:T(8,128)(2,1)S(1)} %bitcast.427), channel_id=1, source_target_pairs={{4,0},{5,1},{6,2},{7,3},{8,4},{9,5},{10,6},{11,7},{12,8},{13,9},{1... | collective-permute-start | bytes 1572872 | tf_op jit(solution)/shard_map/ppermute | solution.py:16
  65.8 7.7 %collective-permute-done.2 = bf16[1,1024,256]{2,1,0:T(8,128)(2,1)S(1)} collective-permute-done((bf16[1,1024,256]{2,1,0:T(8,128)(2,1)S(1)}, bf16[1,1024,256]{2,1,0:T(8,128)(2,1)S(1)}, u32[]{:S(2)}, u32[]{:S(2)}) %collective-permute-start.2) | collective-permute-done | bytes 524320 | tf_op jit(solution)/shard_map/ppermute | solution.py:16
  73.6 4.1 %collective-permute-done.3 = bf16[1,1024,256]{2,1,0:T(8,128)(2,1)S(1)} collective-permute-done((bf16[1,1024,256]{2,1,0:T(8,128)(2,1)S(1)}, bf16[1,1024,256]{2,1,0:T(8,128)(2,1)S(1)}, u32[]{:S(2)}, u32[]{:S(2)}) %collective-permute-start.3) | collective-permute-done | bytes 524320 | tf_op jit(solution)/shard_map/ppermute | solution.py:16
  78.0 0.9 %fusion.8 = bf16[1,16,64,256]{3,2,1,0:T(8,128)(2,1)} fusion(bf16[1,16,64,256]{3,2,1,0:T(8,128)(2,1)S(1)} %bitcast.412, bf16[1,16,64,256]{3,2,1,0:T(8,128)(2,1)S(1)} %fusion.9), kind=kLoop, calls=%fused_computation.61 | loop fusion | flops 1048576 | bytes 1572864 | tf_op jit(solution)/shard_map/convert_element_type | solution.py:93
  (83 shorter events, 16.8 us)
Async XLA Ops:
  0.0 8.3 %copy-start = (bf16[1,16,64,256]{3,2,1,0:T(8,128)(2,1)S(1)}, bf16[1,16,64,256]{3,2,1,0:T(8,128)(2,1)}, u32[]{:S(2)}) copy-start(bf16[1,16,64,256]{3,2,1,0:T(8,128)(2,1)} %param.6) | copy-start | bytes 1572868
  9.0 1.0 %copy-start.1 = (bf16[2,5,5,16,256]{4,3,2,1,0:T(8,128)(2,1)S(1)}, bf16[2,5,5,16,256]{4,3,2,1,0:T(8,128)(2,1)}, u32[]{:S(2)}) copy-start(bf16[2,5,5,16,256]{4,3,2,1,0:T(8,128)(2,1)} %param.7) | copy-start | bytes 1228804
  21.9 0.7 copy-start.3
  22.3 1.2 %copy-start.4 = (bf16[2,1024,256]{2,1,0:T(8,128)(2,1)S(1)}, bf16[2,1024,256]{2,1,0:T(8,128)(2,1)}, u32[]{:S(2)}) copy-start(bf16[2,1024,256]{2,1,0:T(8,128)(2,1)} %param.10) | copy-start | bytes 3145732
  23.5 9.1 %copy-start.2 = (bf16[2,3,256]{2,0,1:T(2,128)(2,1)S(1)}, bf16[2,3,256]{2,0,1:T(2,128)(2,1)}, u32[]{:S(2)}) copy-start(bf16[2,3,256]{2,0,1:T(2,128)(2,1)} %param.11) | copy-start | bytes 9220
  26.1 16.3 %collective-permute-start = (bf16[1,1024,256]{2,1,0:T(8,128)(2,1)S(1)}, bf16[1,1024,256]{2,1,0:T(8,128)(2,1)S(1)}, u32[]{:S(2)}, u32[]{:S(2)}) collective-permute-start(bf16[1,1024,256]{2,1,0:T(8,128)(2,1)S(1)} %bitcast.424), channel_id=1, source_target_pairs={{0,1},{1,2},{2,3},{3,4},{4,5},{5,6},{6,7},{7,8},{8,9},{9,10},{10,1... | collective-permute-start | bytes 1572872 | tf_op jit(solution)/shard_map/ppermute | solution.py:16
  30.7 11.7 %collective-permute-start.1 = (bf16[1,1024,256]{2,1,0:T(8,128)(2,1)S(1)}, bf16[1,1024,256]{2,1,0:T(8,128)(2,1)S(1)}, u32[]{:S(2)}, u32[]{:S(2)}) collective-permute-start(bf16[1,1024,256]{2,1,0:T(8,128)(2,1)S(1)} %bitcast.425), channel_id=1, source_target_pairs={{1,0},{2,1},{3,2},{4,3},{5,4},{6,5},{7,6},{8,7},{9,8},{10,9},{11,1... | collective-permute-start | bytes 1572872 | tf_op jit(solution)/shard_map/ppermute | solution.py:16
  59.7 13.8 %collective-permute-start.2 = (bf16[1,1024,256]{2,1,0:T(8,128)(2,1)S(1)}, bf16[1,1024,256]{2,1,0:T(8,128)(2,1)S(1)}, u32[]{:S(2)}, u32[]{:S(2)}) collective-permute-start(bf16[1,1024,256]{2,1,0:T(8,128)(2,1)S(1)} %bitcast.426), channel_id=1, source_target_pairs={{0,4},{1,5},{2,6},{3,7},{4,8},{5,9},{6,10},{7,11},{8,12},{9,13},{1... | collective-permute-start | bytes 1572872 | tf_op jit(solution)/shard_map/ppermute | solution.py:16
  64.5 13.2 %collective-permute-start.3 = (bf16[1,1024,256]{2,1,0:T(8,128)(2,1)S(1)}, bf16[1,1024,256]{2,1,0:T(8,128)(2,1)S(1)}, u32[]{:S(2)}, u32[]{:S(2)}) collective-permute-start(bf16[1,1024,256]{2,1,0:T(8,128)(2,1)S(1)} %bitcast.427), channel_id=1, source_target_pairs={{4,0},{5,1},{6,2},{7,3},{8,4},{9,5},{10,6},{11,7},{12,8},{13,9},{1... | collective-permute-start | bytes 1572872 | tf_op jit(solution)/shard_map/ppermute | solution.py:16
where the time goes:
time: 79.3 us; the launch traced here: 79 us
  local copies, waits for them, and re-layouts  27.2 us (34%)
  waiting for transfers between devices  19.7 us (25%)
  matrix products  13.3 us (17%)
  starting transfers between devices  12.5 us (16%)
  other arithmetic  5.53 us (7%)
    unnamed x54, local copies, waits for them, and re-layouts  21.6 us
    ppermute x4, waiting for transfers between devices, shifted(): return lax.ppermute(block, axis, route)  19.7 us
    ppermute x4, starting transfers between devices, shifted(): return lax.ppermute(block, axis, route)  12.5 us
    unnamed x10, matrix products  8.31 us
    dot_general x2, matrix products, shards(): jnp.dot(hidden, down_weight[layer_number], preferred_element_type=jnp.flo...  5.02 us
    select_n x1, other arithmetic, dense_taps(): jnp.where(row_group == column_cluster, tiled_taps, jnp.zeros_like(tiled_t...  2.11 us
    concatenate x8, local copies, waits for them, and re-layouts, plane_conv(): window = jnp.concatenate(pieces, axis=-1)  2.1 us
    another operation x2, local copies, waits for them, and re-layouts, dense_taps(): jnp.stack([masked[:, :, index_b * block_size:(index_b + 1) * block_size,...  2.03 us
  transfers between devices with their start and end apart: 4, of which 3 were waited for; matrix products, arithmetic and copies ran while one was open for 2% of the time, Pallas kernels for 0%

commit v1 on v0

v1 whole, which is shorter than its diff:
```python
import functools

import jax
import jax.numpy as jnp
from jax import lax
from jax.experimental import pallas as pl
from jax.experimental.pallas import tpu as pltpu
from jax.sharding import PartitionSpec as P

DILATIONS = (1, 4)
TAPS = 5
EPSILON = 1e-06
CHUNK_X = 4


def kernel(devices, extent_x, extent_y, vol_hbm, plane_hbm, gain_ref, expand_hbm, down_hbm, depth_ref, out_hbm,
           cur, plane, expand, down, mask, taps, window, mixed, lower, upper, result,
           load_sem, send_sem, recv_sem, out_sem):
    me = lax.axis_index("slab")
    channels = cur.shape[1]
    group = plane.shape[0] // (2 * TAPS * TAPS)
    rows = CHUNK_X * extent_y
    chunks = extent_x // CHUNK_X
    halo = 2 * extent_y
    hid = expand.shape[1]

    loads = [
        pltpu.make_async_copy(src, dst, load_sem.at[k])
        for k, (src, dst) in enumerate(
            ((plane_hbm, plane), (vol_hbm, cur), (expand_hbm, expand), (down_hbm, down)))
    ]
    for load in loads:
        load.start()

    reach = [(layer, side, me + (d if side == 0 else -d))
             for layer, d in enumerate(DILATIONS) for side in (0, 1)]

    def inside(other):
        return jnp.logical_and(other >= 0, other < devices)

    barrier = pltpu.get_barrier_semaphore()
    for _, _, other in reach:
        @pl.when(inside(other))
        def _():
            pl.semaphore_signal(barrier, inc=1, device_id={"slab": other}, device_id_type=pl.DeviceIdType.MESH)

    row_group = lax.broadcasted_iota(jnp.int32, (channels, channels), 0) // group
    column_group = lax.broadcasted_iota(jnp.int32, (channels, channels), 1) // group
    mask[...] = jnp.where(row_group == column_group, 1.0, 0.0).astype(jnp.bfloat16)
    edge = jnp.zeros((halo, TAPS * channels), jnp.bfloat16)
    window[:halo, :] = edge
    window[halo + extent_x * extent_y:, :] = edge

    for layer, side, other in reach:
        source = me - (other - me)
        landing = lower if side == 0 else upper

        @pl.when(jnp.logical_not(inside(source)))
        def _():
            landing[layer] = jnp.zeros(landing.shape[1:], jnp.bfloat16)

    def build_taps(layer):
        def one(t, carry):
            tap = plane[pl.ds(pl.multiple_of((layer * TAPS * TAPS + t) * group, group), group), :]
            tiled = jnp.concatenate([tap] * (channels // group), axis=0)
            taps[pl.ds(pl.multiple_of(t * channels, channels), channels), :] = tiled * mask[...]
            return carry
        lax.fori_loop(0, TAPS * TAPS, one, 0)

    def fill(at, value):
        y = lax.broadcasted_iota(jnp.int32, (rows, channels), 0) % extent_y
        for dy in range(TAPS):
            shift = dy - 2
            if shift == 0:
                moved = value
            else:
                moved = pltpu.roll(value, (-shift) % rows, 0)
                inside_y = jnp.logical_and(y + shift >= 0, y + shift < extent_y)
                moved = jnp.where(inside_y, moved, 0.0)
            window[pl.ds(at + halo, rows), dy * channels:(dy + 1) * channels] = moved.astype(jnp.bfloat16)

    def mix(layer, at):
        total = None
        for dx in range(TAPS):
            part = jnp.dot(
                window[pl.ds(pl.multiple_of(at + dx * extent_y, extent_y), rows), :],
                taps[dx * TAPS * channels:(dx + 1) * TAPS * channels, :],
                preferred_element_type=jnp.float32)
            total = part if total is None else total + part
        scale = lax.rsqrt(jnp.mean(total * total, axis=-1, keepdims=True) + EPSILON)
        gain = gain_ref[...].astype(jnp.float32)[layer:layer + 1] * 0.5
        half = (total * scale * gain).astype(jnp.bfloat16)
        h = jnp.dot(half, expand[layer * channels:(layer + 1) * channels, :], preferred_element_type=jnp.float32)
        hidden = (h + h * jnp.tanh(h)).astype(jnp.bfloat16)
        out = jnp.dot(hidden, down[layer * hid:(layer + 1) * hid, :], preferred_element_type=jnp.float32)
        mixed[layer, pl.ds(at, rows), :] = out.astype(jnp.bfloat16)

    def copy(layer, side, chunk):
        at = pl.multiple_of(chunk * rows, rows)
        landing = lower if side == 0 else upper
        d = DILATIONS[layer]
        return pltpu.make_async_remote_copy(
            src_ref=mixed.at[layer, pl.ds(at, rows), :],
            dst_ref=landing.at[layer, pl.ds(at, rows), :],
            send_sem=send_sem.at[layer, side, chunk],
            recv_sem=recv_sem.at[layer, side, chunk],
            device_id={"slab": me + (d if side == 0 else -d)},
            device_id_type=pl.DeviceIdType.MESH)

    def send(layer, chunk):
        for side in (0, 1):
            d = DILATIONS[layer]

            @pl.when(inside(me + (d if side == 0 else -d)))
            def _():
                copy(layer, side, chunk).start()

    def receive(layer, chunk):
        for side in (0, 1):
            d = DILATIONS[layer]

            @pl.when(inside(me - (d if side == 0 else -d)))
            def _():
                copy(layer, side, chunk).wait_recv()

    def combine(layer, at):
        coeffs = depth_ref[layer].astype(jnp.float32)
        here = pl.ds(at, rows)
        term = (coeffs[0:1] * lower[layer, here, :].astype(jnp.float32)
                + coeffs[1:2] * mixed[layer, here, :].astype(jnp.float32)
                + coeffs[2:3] * upper[layer, here, :].astype(jnp.float32))
        term = term.astype(jnp.bfloat16).astype(jnp.float32)
        return (cur[here, :].astype(jnp.float32) + term).astype(jnp.bfloat16)

    loads[0].wait()
    build_taps(0)
    loads[1].wait()

    def first_fill(i, carry):
        at = pl.multiple_of(i * rows, rows)
        fill(at, cur[pl.ds(at, rows), :].astype(jnp.float32))
        return carry
    lax.fori_loop(0, chunks, first_fill, 0)
    loads[2].wait()
    loads[3].wait()
    pl.semaphore_wait(barrier, sum(inside(other).astype(jnp.int32) for _, _, other in reach))

    def first(i, carry):
        mix(0, pl.multiple_of(i * rows, rows))
        send(0, i)
        return carry
    lax.fori_loop(0, chunks, first, 0)

    build_taps(1)

    def second(i, carry):
        @pl.when(i < chunks)
        def _():
            receive(0, i)
            at = pl.multiple_of(i * rows, rows)
            value = combine(0, at)
            cur[pl.ds(at, rows), :] = value
            fill(at, value.astype(jnp.float32))

        @pl.when(i >= 1)
        def _():
            mix(1, pl.multiple_of((i - 1) * rows, rows))
            send(1, i - 1)
        return carry
    lax.fori_loop(0, chunks + 1, second, 0)

    def store(i):
        at = pl.multiple_of(i * rows, rows)
        return pltpu.make_async_copy(result.at[pl.ds(at, rows), :], out_hbm.at[pl.ds(at, rows), :], out_sem.at[i])

    def last(i, carry):
        receive(1, i)
        at = pl.multiple_of(i * rows, rows)
        result[pl.ds(at, rows), :] = combine(1, at)
        store(i).start()
        return carry
    lax.fori_loop(0, chunks, last, 0)

    def drain(i, carry):
        store(i).wait()
        for layer, side, other in reach:
            @pl.when(inside(other))
            def _():
                copy(layer, side, i).wait_send()
        return carry
    lax.fori_loop(0, chunks, drain, 0)


def shards(devices, volume, plane_weight, norm_gain, expand_weight, down_weight, depth_weight):
    slab_depth, extent_x, extent_y, channels = volume.shape
    layers, _, _, group, _ = plane_weight.shape
    hid = expand_weight.shape[2]
    cells = extent_x * extent_y
    chunks = extent_x // CHUNK_X
    bf16 = jnp.bfloat16
    whole = pl.BlockSpec(memory_space=pltpu.VMEM)
    far = pl.BlockSpec(memory_space=pl.ANY)
    out = pl.pallas_call(
        functools.partial(kernel, devices, extent_x, extent_y),
        out_shape=jax.ShapeDtypeStruct((cells, channels), bf16),
        in_specs=[far, far, whole, far, far, whole],
        out_specs=far,
        scratch_shapes=[
            pltpu.VMEM((cells, channels), bf16),
            pltpu.VMEM((layers * TAPS * TAPS * group, channels), bf16),
            pltpu.VMEM((layers * channels, hid), bf16),
            pltpu.VMEM((layers * hid, channels), bf16),
            pltpu.VMEM((channels, channels), bf16),
            pltpu.VMEM((TAPS * TAPS * channels, channels), bf16),
            pltpu.VMEM((cells + 4 * extent_y, TAPS * channels), bf16),
            pltpu.VMEM((layers, cells, channels), bf16),
            pltpu.VMEM((layers, cells, channels), bf16),
            pltpu.VMEM((layers, cells, channels), bf16),
            pltpu.VMEM((cells, channels), bf16),
            pltpu.SemaphoreType.DMA((4,)),
            pltpu.SemaphoreType.DMA((layers, 2, chunks)),
            pltpu.SemaphoreType.DMA((layers, 2, chunks)),
            pltpu.SemaphoreType.DMA((chunks,)),
        ],
        compiler_params=pltpu.CompilerParams(
            collective_id=0, has_side_effects=True, vmem_limit_bytes=48 * 1024 * 1024),
        cost_estimate=pl.CostEstimate(flops=9 * 10**9, bytes_accessed=5 * 10**6, transcendentals=2 * 10**6),
    )(
        volume.reshape(cells, channels),
        plane_weight.reshape(layers * TAPS * TAPS * group, channels),
        norm_gain,
        expand_weight.reshape(layers * channels, hid),
        down_weight.reshape(layers * hid, channels),
        depth_weight,
    )
    return out.reshape(volume.shape)


def solution(mesh):
    placed = (P(("parts", "slab"), None, None, None), P(), P(), P(), P(), P())
    return jax.shard_map(
        functools.partial(shards, mesh.shape["slab"]),
        mesh=mesh,
        in_specs=placed,
        out_specs=P(("parts", "slab"), None, None, None),
        check_vma=False,
    )
```

time: 79.3 us -> 36.3 us (0.46)
  Pallas kernels: 0 us -> 29.3 us
  local copies, waits for them, and re-layouts: 27.2 us -> 6.65 us
  waiting for transfers between devices: 19.7 us -> 0 us
  matrix products: 13.3 us -> 0 us
  starting transfers between devices: 12.5 us -> 0 us
  other arithmetic: 5.53 us -> 0 us
    pallas_call x0 -> x1, Pallas kernels: none -> 29.3 us  [shards(): pl.pallas_call(functools.partial(kernel, devices, extent_x, extent_y), ou...]
    ppermute x4 -> x0, waiting for transfers between devices: 19.7 us -> none  [shifted(): return lax.ppermute(block, axis, route)]
    unnamed x54 -> x14, local copies, waits for them, and re-layouts: 21.6 us -> 6.65 us
    ppermute x4 -> x0, starting transfers between devices: 12.5 us -> none  [shifted(): return lax.ppermute(block, axis, route)]
    unnamed x10 -> x0, matrix products: 8.31 us -> none
    dot_general x2 -> x0, matrix products: 5.02 us -> none  [shards(): jnp.dot(hidden, down_weight[layer_number], preferred_element_type=jnp.flo...]
    convert_element_type x8 -> x0, other arithmetic: 2.2 us -> none  [the longest x2 1.11 us: shards(): current = (current.astype(jnp.float32) + returned.reshape(current.shape)....]
    select_n x2 -> x0, other arithmetic: 2.11 us -> none  [the longest x1 2.11 us: dense_taps(): jnp.where(row_group == column_cluster, tiled_taps, jnp.zeros_like(tiled_t...]
  transfers between devices with their start and end apart: 4 -> 0, of which waited for: 3 -> 0; matrix products, arithmetic and copies ran while one was open for 2% -> 0% of each run, Pallas kernels for 0% -> 0%
where the time goes in v1:
time: 36.3 us; the launch traced here: 36 us
  Pallas kernels  29.3 us (81%)
  local copies, waits for them, and re-layouts  6.65 us (18%)
    pallas_call x1, Pallas kernels, shards(): pl.pallas_call(functools.partial(kernel, devices, extent_x, extent_y), ou...  29.3 us
    unnamed x14, local copies, waits for them, and re-layouts  6.65 us

profile of v1, /device:TPU:1, one launch (start us, length us, event | category | flops | bytes accessed | tf_op | source)
XLA Modules:
  0.0 36.0 jit_solution(3776219405278418012)
XLA Ops:
  0.0 0.0 copy-start.5
  0.0 0.7 %copy-done.5 = bf16[2,3,256]{2,0,1:T(2,128)(2,1)S(1)} copy-done((bf16[2,3,256]{2,0,1:T(2,128)(2,1)S(1)}, bf16[2,3,256]{2,0,1:T(2,128)(2,1)}, u32[]{:S(2)}) %copy-start.5) | copy-done | bytes 3096
  0.7 0.0 copy-start.4
  0.7 0.7 %copy-done.4 = bf16[2,256]{1,0:T(2,128)(2,1)S(1)} copy-done((bf16[2,256]{1,0:T(2,128)(2,1)S(1)}, bf16[2,256]{1,0:T(2,128)(2,1)}, u32[]{:S(2)}) %copy-start.4) | copy-done | bytes 1048
  1.4 0.0 copy-start
  1.4 1.2 %copy-done = bf16[2,256,1024]{2,1,0:T(8,128)(2,1)S(1)} copy-done((bf16[2,256,1024]{2,1,0:T(8,128)(2,1)S(1)}, bf16[2,256,1024]{2,1,0:T(8,128)(2,1)}, u32[]{:S(2)}) %copy-start) | copy-done | bytes 1048600
  2.6 0.0 copy-start.1
  2.6 1.2 %copy-done.1 = bf16[2,1024,256]{2,1,0:T(8,128)(2,1)S(1)} copy-done((bf16[2,1024,256]{2,1,0:T(8,128)(2,1)S(1)}, bf16[2,1024,256]{2,1,0:T(8,128)(2,1)}, u32[]{:S(2)}) %copy-start.1) | copy-done | bytes 1048600
  3.8 0.0 copy-start.2
  3.8 1.0 %copy-done.2 = bf16[1,16,64,256]{3,2,1,0:T(8,128)(2,1)S(1)} copy-done((bf16[1,16,64,256]{3,2,1,0:T(8,128)(2,1)S(1)}, bf16[1,16,64,256]{3,2,1,0:T(8,128)(2,1)}, u32[]{:S(2)}) %copy-start.2) | copy-done | bytes 524312
  4.9 0.0 copy-start.3
  4.9 1.0 %copy-done.3 = bf16[2,5,5,16,256]{4,3,2,1,0:T(8,128)(2,1)S(1)} copy-done((bf16[2,5,5,16,256]{4,3,2,1,0:T(8,128)(2,1)S(1)}, bf16[2,5,5,16,256]{4,3,2,1,0:T(8,128)(2,1)}, u32[]{:S(2)}) %copy-start.3) | copy-done | bytes 409624
  5.9 29.3 %shard_map.64 = bf16[1024,256]{1,0:T(8,128)(2,1)S(1)} custom-call(bf16[1024,256]{1,0:T(8,128)(2,1)S(1)} %bitcast.8, bf16[800,256]{1,0:T(8,128)(2,1)S(1)} %bitcast.9, bf16[2,256]{1,0:T(2,128)(2,1)S(1)} %copy-done.4, bf16[512,1024]{1,0:T(8,128)(2,1)S(1)} %bitcast.6, bf16[2048,256]{1,0:T(8,128)(2,1)S(1)} %bitcast.7, bf16[2,3,256]{2,1,0:T(4,128)(2,1)S(1)} %copy.7.depth_ref), custom_call_target="tpu_custom_call" | custom-call | flops 8999999488 | bytes 5000000 | tf_op jit(solution)/shard_map/pallas_call | solution.py:203
  35.2 0.8 %copy.9 = bf16[1,16,64,256]{3,2,1,0:T(8,128)(2,1)} copy(bf16[1,16,64,256]{3,2,1,0:T(8,128)(2,1)S(1)} %bitcast.5) | data formatting | bytes 1048576
  (1 shorter events, 0.0 us)
Async XLA Ops:
  0.0 0.7 %copy-start.5 = (bf16[2,3,256]{2,0,1:T(2,128)(2,1)S(1)}, bf16[2,3,256]{2,0,1:T(2,128)(2,1)}, u32[]{:S(2)}) copy-start(bf16[2,3,256]{2,0,1:T(2,128)(2,1)} %param.11) | copy-start | bytes 9220
  0.7 0.7 %copy-start.4 = (bf16[2,256]{1,0:T(2,128)(2,1)S(1)}, bf16[2,256]{1,0:T(2,128)(2,1)}, u32[]{:S(2)}) copy-start(bf16[2,256]{1,0:T(2,128)(2,1)} %gain_ref.1) | copy-start | bytes 3076
  1.4 1.2 %copy-start = (bf16[2,256,1024]{2,1,0:T(8,128)(2,1)S(1)}, bf16[2,256,1024]{2,1,0:T(8,128)(2,1)}, u32[]{:S(2)}) copy-start(bf16[2,256,1024]{2,1,0:T(8,128)(2,1)} %param.9) | copy-start | bytes 3145732
  2.6 1.2 %copy-start.1 = (bf16[2,1024,256]{2,1,0:T(8,128)(2,1)S(1)}, bf16[2,1024,256]{2,1,0:T(8,128)(2,1)}, u32[]{:S(2)}) copy-start(bf16[2,1024,256]{2,1,0:T(8,128)(2,1)} %param.10) | copy-start | bytes 3145732
  3.8 1.0 %copy-start.2 = (bf16[1,16,64,256]{3,2,1,0:T(8,128)(2,1)S(1)}, bf16[1,16,64,256]{3,2,1,0:T(8,128)(2,1)}, u32[]{:S(2)}) copy-start(bf16[1,16,64,256]{3,2,1,0:T(8,128)(2,1)} %param.6) | copy-start | bytes 1572868
  4.9 1.0 %copy-start.3 = (bf16[2,5,5,16,256]{4,3,2,1,0:T(8,128)(2,1)S(1)}, bf16[2,5,5,16,256]{4,3,2,1,0:T(8,128)(2,1)}, u32[]{:S(2)}) copy-start(bf16[2,5,5,16,256]{4,3,2,1,0:T(8,128)(2,1)} %param.7) | copy-start | bytes 1228804

commit v2 on v1

--- a/solution.py
+++ b/solution.py
@@ -124,11 +124,11 @@
                 copy(layer, side, chunk).wait_recv()
 
     def combine(layer, at):
-        coeffs = depth_ref[layer].astype(jnp.float32)
+        coeffs = [depth_ref[k].astype(jnp.float32)[layer:layer + 1] for k in range(3)]
         here = pl.ds(at, rows)
-        term = (coeffs[0:1] * lower[layer, here, :].astype(jnp.float32)
-                + coeffs[1:2] * mixed[layer, here, :].astype(jnp.float32)
-                + coeffs[2:3] * upper[layer, here, :].astype(jnp.float32))
+        term = (coeffs[0] * lower[layer, here, :].astype(jnp.float32)
+                + coeffs[1] * mixed[layer, here, :].astype(jnp.float32)
+                + coeffs[2] * upper[layer, here, :].astype(jnp.float32))
         term = term.astype(jnp.bfloat16).astype(jnp.float32)
         return (cur[here, :].astype(jnp.float32) + term).astype(jnp.bfloat16)
 
@@ -223,7 +223,7 @@
             pltpu.SemaphoreType.DMA((chunks,)),
         ],
         compiler_params=pltpu.CompilerParams(
-            collective_id=0, has_side_effects=True, vmem_limit_bytes=48 * 1024 * 1024),
+            collective_id=0, has_side_effects=True, vmem_limit_bytes=63 * 1024 * 1024),
         cost_estimate=pl.CostEstimate(flops=9 * 10**9, bytes_accessed=5 * 10**6, transcendentals=2 * 10**6),
     )(
         volume.reshape(cells, channels),
@@ -231,7 +231,7 @@
         norm_gain,
         expand_weight.reshape(layers * channels, hid),
         down_weight.reshape(layers * hid, channels),
-        depth_weight,
+        depth_weight.transpose(1, 0, 2),
     )
     return out.reshape(volume.shape)
 

time: 36.3 us -> 32.4 us (0.89)
  local copies, waits for them, and re-layouts: 6.65 us -> 1.88 us
  Pallas kernels: 29.3 us -> 30.3 us
    unnamed x14 -> x1, local copies, waits for them, and re-layouts: 6.65 us -> 1.88 us
    pallas_call x1, Pallas kernels: 29.3 us -> 30.3 us  [shards(): pl.pallas_call(functools.partial(kernel, devices, extent_x, extent_y), ou...]
where the time goes in v2:
time: 32.4 us; the launch traced here: 32.2 us
  Pallas kernels  30.3 us (94%)
  local copies, waits for them, and re-layouts  1.88 us (6%)
    pallas_call x1, Pallas kernels, shards(): pl.pallas_call(functools.partial(kernel, devices, extent_x, extent_y), ou...  30.3 us
    unnamed x1, local copies, waits for them, and re-layouts  1.88 us

profile of v2, /device:TPU:1, one launch (start us, length us, event | category | flops | bytes accessed | tf_op | source)
XLA Modules:
  0.0 32.2 jit_solution(493629099101157226)
XLA Ops:
  0.0 30.3 %shard_map.64 = bf16[1024,256]{1,0:T(8,128)(2,1)} custom-call(bf16[1024,256]{1,0:T(8,128)(2,1)} %bitcast.9, bf16[800,256]{1,0:T(8,128)(2,1)} %bitcast.10, bf16[2,256]{1,0:T(2,128)(2,1)} %gain_ref.1, bf16[512,1024]{1,0:T(8,128)(2,1)} %bitcast.7, bf16[2048,256]{1,0:T(8,128)(2,1)} %bitcast.8, bf16[3,2,256]{2,1,0:T(2,128)(2,1)} %bitcast.11), custom_call_target="tpu_custom_call" | custom-call | flops 8999999488 | bytes 5000000 | tf_op jit(solution)/shard_map/pallas_call | solution.py:203
  30.3 1.9 %copy.8 = bf16[1,16,64,256]{3,2,1,0:T(8,128)(2,1)} copy(bf16[1,16,64,256]{3,2,1,0:T(8,128)(2,1)} %bitcast.6) | data formatting | bytes 1048576

commit v3 on v2

v3 whole, which is shorter than its diff:
```python
import functools

import jax
import jax.numpy as jnp
from jax import lax
from jax.experimental import pallas as pl
from jax.experimental.pallas import tpu as pltpu
from jax.sharding import PartitionSpec as P

DILATIONS = (1, 4)
TAPS = 5
EPSILON = 1e-06
CHUNK_X = 4
PACK = 4
CONV_CHUNKS = 2


def kernel(devices, extent_x, extent_y, vol_hbm, plane_hbm, gain_ref, expand_hbm, down_hbm, depth_ref, out_hbm,
           vol, stage, cur, plane, expand, down, taps, window, normed, mixed, lower, upper, result,
           load_sem, send_sem, recv_sem, out_sem):
    me = lax.axis_index("slab")
    channels = cur.shape[1]
    group = plane.shape[0] // (2 * TAPS * TAPS)
    blocks = extent_y // PACK
    plane_rows = CHUNK_X * blocks
    rows = PACK * plane_rows
    chunks = extent_x // CHUNK_X
    halo = 2 * blocks
    hid = expand.shape[1]
    half = channels // 2
    quarter = channels // PACK
    depth = 2 * channels
    bf16, f32 = jnp.bfloat16, jnp.float32

    loads = [
        pltpu.make_async_copy(src, dst, load_sem.at[k])
        for k, (src, dst) in enumerate(
            ((plane_hbm, plane), (vol_hbm, vol), (expand_hbm, expand), (down_hbm, down)))
    ]
    for load in loads:
        load.start()

    reach = [(layer, side, me + (d if side == 0 else -d))
             for layer, d in enumerate(DILATIONS) for side in (0, 1)]

    def inside(other):
        return jnp.logical_and(other >= 0, other < devices)

    barrier = pltpu.get_barrier_semaphore()
    for _, _, other in reach:
        @pl.when(inside(other))
        def _():
            pl.semaphore_signal(barrier, inc=1, device_id={"slab": other}, device_id_type=pl.DeviceIdType.MESH)

    edge = jnp.zeros((halo, PACK * depth), bf16)
    window[:halo, :] = edge
    window[halo + extent_x * blocks:, :] = edge

    for layer, side, other in reach:
        source = me - (other - me)
        landing = lower if side == 0 else upper

        @pl.when(jnp.logical_not(inside(source)))
        def _():
            landing[layer] = jnp.zeros(landing.shape[1:], bf16)

    def is_low(count):
        return lax.broadcasted_iota(jnp.int32, (count, half), 1) < quarter

    def swap(value):
        return pltpu.roll(value, quarter, 1)

    lane_group = lax.broadcasted_iota(jnp.int32, (group, half), 1) % quarter // group
    group_mask = [jnp.where(lane_group == g, 1.0, 0.0).astype(bf16) for g in range(quarter // group)]

    def clear(t, carry):
        for v, start in ((0, 6 * quarter), (1, 0)):
            taps[pl.ds(pl.multiple_of(t * depth + start, 2 * quarter), 2 * quarter), v * half:(v + 1) * half] = (
                jnp.zeros((2 * quarter, half), bf16))
        return carry
    lax.fori_loop(0, TAPS * PACK, clear, 0)

    def build_taps(layer):
        def one(dx, carry):
            base = (layer * TAPS + dx) * TAPS * group
            for h in range(2):
                straight = [
                    plane[pl.ds(pl.multiple_of(base + dy * group, group), group), h * half:(h + 1) * half].astype(f32)
                    for dy in range(TAPS)]
                swapped = [swap(value) for value in straight]
                zero = jnp.zeros((group, half), f32)
                for odd in range(2):
                    left, right = (swapped, straight) if odd else (straight, swapped)
                    at = pl.multiple_of((dx * PACK + 2 * h + odd) * depth, depth)
                    for k in range(TAPS + 1):
                        pair = jnp.where(
                            is_low(group), left[k] if k < TAPS else zero, right[k - 1] if k > 0 else zero).astype(bf16)
                        for g, only in enumerate(group_mask):
                            tile = pair * only
                            for v in range(2):
                                taps[pl.ds(at + (k + 2 * v) * quarter + g * group, group),
                                     v * half:(v + 1) * half] = tile
            return carry
        lax.fori_loop(0, TAPS, one, 0)

    def fill(chunk, planes):
        block = lax.broadcasted_iota(jnp.int32, (plane_rows, channels), 0) % blocks

        def before(value):
            return jnp.where(block == 0, 0.0, pltpu.roll(value, 1, 0))

        def after(value):
            return jnp.where(block == blocks - 1, 0.0, pltpu.roll(value, plane_rows - 1, 0))

        y = [before(planes[2]), before(planes[3]), *planes, after(planes[0]), after(planes[1])]
        here = pl.ds(pl.multiple_of(chunk * plane_rows + halo, halo), plane_rows)
        low = is_low(plane_rows)
        for k in range(0, 2 * PACK, 2):
            for h in range(2):
                a = y[k][:, h * half:(h + 1) * half]
                b = y[k + 1][:, h * half:(h + 1) * half]
                at = 2 * h * depth + k * quarter
                window[here, at:at + half] = jnp.where(low, a, swap(b)).astype(bf16)
                window[here, at + depth:at + depth + half] = jnp.where(low, swap(a), b).astype(bf16)

    ones = jnp.where(
        lax.broadcasted_iota(jnp.int32, (channels, channels), 0) // quarter
        == lax.broadcasted_iota(jnp.int32, (channels, channels), 1) // quarter, 1.0, 0.0).astype(bf16)

    def conv(layer, first_chunk, count):
        size = count * plane_rows
        at = first_chunk * plane_rows
        totals = []
        for q in range(PACK):
            total = None
            for dx in range(TAPS):
                part = jnp.dot(
                    window[at + dx * blocks:at + dx * blocks + size, q * depth:(q + 1) * depth],
                    taps[(dx * PACK + q) * depth:(dx * PACK + q + 1) * depth, :],
                    preferred_element_type=f32)
                total = part if total is None else total + part
            totals.append(total)
        squares = sum(total * total for total in totals)
        coarse = squares.astype(bf16)
        fine = (squares - coarse.astype(f32)).astype(bf16)
        mean = (jnp.dot(coarse, ones, preferred_element_type=f32)
                + jnp.dot(fine, ones, preferred_element_type=f32)) * (1.0 / channels)
        scale = lax.rsqrt(mean + EPSILON)
        gain = gain_ref[...].astype(f32)[layer:layer + 1] * 0.5
        low = is_low(size)
        for h in range(2):
            pair = gain[:, h * half:(h + 1) * half]
            other = swap(jnp.broadcast_to(pair, (8, half)))[0:1]
            low_row = is_low(1)
            even = jnp.where(low_row, pair, other)
            odd = jnp.where(low_row, other, pair)
            for v in range(2):
                lanes = slice(v * half, (v + 1) * half)
                a = totals[2 * h][:, lanes] * scale[:, lanes] * even
                b = totals[2 * h + 1][:, lanes] * scale[:, lanes] * odd
                for j, value in ((2 * v, jnp.where(low, a, swap(b))), (2 * v + 1, jnp.where(low, swap(a), b))):
                    value = value.astype(bf16)
                    for c in range(count):
                        to = (first_chunk + c) * rows + j * plane_rows
                        normed[to:to + plane_rows, h * half:(h + 1) * half] = (
                            value[c * plane_rows:(c + 1) * plane_rows])

    def mix(layer, chunk):
        here = pl.ds(pl.multiple_of(chunk * rows, rows), rows)
        h = jnp.dot(normed[here, :], expand[layer * channels:(layer + 1) * channels, :],
                    preferred_element_type=f32).astype(bf16)
        hidden = h + h * jnp.tanh(h)
        out = jnp.dot(hidden, down[layer * hid:(layer + 1) * hid, :], preferred_element_type=f32)
        mixed[layer, here, :] = out.astype(bf16)

    def copy(layer, side, chunk):
        at = pl.multiple_of(chunk * rows, rows)
        landing = lower if side == 0 else upper
        d = DILATIONS[layer]
        return pltpu.make_async_remote_copy(
            src_ref=mixed.at[layer, pl.ds(at, rows), :],
            dst_ref=landing.at[layer, pl.ds(at, rows), :],
            send_sem=send_sem.at[layer, side, chunk],
            recv_sem=recv_sem.at[layer, side, chunk],
            device_id={"slab": me + (d if side == 0 else -d)},
            device_id_type=pl.DeviceIdType.MESH)

    def send(layer, chunk):
        for side in (0, 1):
            d = DILATIONS[layer]

            @pl.when(inside(me + (d if side == 0 else -d)))
            def _():
                copy(layer, side, chunk).start()

    def receive(layer, chunk):
        for side in (0, 1):
            d = DILATIONS[layer]

            @pl.when(inside(me - (d if side == 0 else -d)))
            def _():
                copy(layer, side, chunk).wait_recv()

    def combine(layer, at):
        coeffs = [depth_ref[k].astype(f32)[layer:layer + 1] for k in range(3)]
        here = pl.ds(at, rows)
        term = (coeffs[0] * lower[layer, here, :].astype(f32)
                + coeffs[1] * mixed[layer, here, :].astype(f32)
                + coeffs[2] * upper[layer, here, :].astype(f32))
        term = term.astype(bf16).astype(f32)
        return (cur[here, :].astype(f32) + term).astype(bf16).astype(f32)

    def mix_and_send(layer, first_chunk, count):
        def one(i, carry):
            mix(layer, i)
            send(layer, i)
            return carry
        lax.fori_loop(first_chunk, first_chunk + count, one, 0)

    loads[1].wait()

    def first_fill(i, carry):
        at = pl.multiple_of(i * rows, rows)
        value = vol[pl.ds(at, rows), :].astype(f32)
        for h in range(2):
            stage[h, pl.ds(at, rows), :] = value[:, h * half:(h + 1) * half]
        planes = [
            jnp.concatenate([stage[h, pl.ds(at + j, plane_rows, stride=PACK), :] for h in range(2)], axis=1)
            for j in range(PACK)]
        for j in range(PACK):
            cur[pl.ds(at + j * plane_rows, plane_rows), :] = planes[j].astype(bf16)
        fill(i, planes)
        return carry
    lax.fori_loop(0, chunks, first_fill, 0)
    loads[0].wait()
    build_taps(0)
    conv(0, 0, chunks)
    loads[2].wait()
    loads[3].wait()
    pl.semaphore_wait(barrier, sum(inside(other).astype(jnp.int32) for _, _, other in reach))
    mix_and_send(0, 0, chunks)

    build_taps(1)

    def refill(i, carry):
        receive(0, i)
        at = pl.multiple_of(i * rows, rows)
        value = combine(0, at)
        cur[pl.ds(at, rows), :] = value.astype(bf16)
        fill(i, [value[j * plane_rows:(j + 1) * plane_rows] for j in range(PACK)])
        return carry

    filled = 0
    for start in range(0, chunks, CONV_CHUNKS):
        need = min(start + CONV_CHUNKS + 1, chunks)
        lax.fori_loop(filled, need, refill, 0)
        filled = need
        conv(1, start, CONV_CHUNKS)
        mix_and_send(1, start, CONV_CHUNKS)

    def store(i):
        at = pl.multiple_of(i * rows, rows)
        return pltpu.make_async_copy(result.at[pl.ds(at, rows), :], out_hbm.at[pl.ds(at, rows), :], out_sem.at[i])

    def last(i, carry):
        receive(1, i)
        at = pl.multiple_of(i * rows, rows)
        value = combine(1, at)
        for h in range(2):
            for j in range(PACK):
                stage[h, pl.ds(at + j, plane_rows, stride=PACK), :] = (
                    value[j * plane_rows:(j + 1) * plane_rows, h * half:(h + 1) * half])
            result[pl.ds(at, rows), h * half:(h + 1) * half] = stage[h, pl.ds(at, rows), :].astype(bf16)
        store(i).start()
        return carry
    lax.fori_loop(0, chunks, last, 0)

    def drain(i, carry):
        store(i).wait()
        for layer, side, other in reach:
            @pl.when(inside(other))
            def _():
                copy(layer, side, i).wait_send()
        return carry
    lax.fori_loop(0, chunks, drain, 0)


def shards(devices, volume, plane_weight, norm_gain, expand_weight, down_weight, depth_weight):
    slab_depth, extent_x, extent_y, channels = volume.shape
    layers, _, _, group, _ = plane_weight.shape
    hid = expand_weight.shape[2]
    cells = extent_x * extent_y
    chunks = extent_x // CHUNK_X
    bf16 = jnp.bfloat16
    whole = pl.BlockSpec(memory_space=pltpu.VMEM)
    far = pl.BlockSpec(memory_space=pl.ANY)
    out = pl.pallas_call(
        functools.partial(kernel, devices, extent_x, extent_y),
        out_shape=jax.ShapeDtypeStruct((cells, channels), bf16),
        in_specs=[far, far, whole, far, far, whole],
        out_specs=far,
        scratch_shapes=[
            pltpu.VMEM((cells, channels), bf16),
            pltpu.VMEM((2, cells, channels // 2), jnp.float32),
            pltpu.VMEM((cells, channels), bf16),
            pltpu.VMEM((layers * TAPS * TAPS * group, channels), bf16),
            pltpu.VMEM((layers * channels, hid), bf16),
            pltpu.VMEM((layers * hid, channels), bf16),
            pltpu.VMEM((TAPS * PACK * 2 * channels, channels), bf16),
            pltpu.VMEM(((extent_x + 4) * extent_y // PACK, PACK * 2 * channels), bf16),
            pltpu.VMEM((cells, channels), bf16),
            pltpu.VMEM((layers, cells, channels), bf16),
            pltpu.VMEM((layers, cells, channels), bf16),
            pltpu.VMEM((layers, cells, channels), bf16),
            pltpu.VMEM((cells, channels), bf16),
            pltpu.SemaphoreType.DMA((4,)),
            pltpu.SemaphoreType.DMA((layers, 2, chunks)),
            pltpu.SemaphoreType.DMA((layers, 2, chunks)),
            pltpu.SemaphoreType.DMA((chunks,)),
        ],
        compiler_params=pltpu.CompilerParams(
            collective_id=0, has_side_effects=True, vmem_limit_bytes=63 * 1024 * 1024),
        cost_estimate=pl.CostEstimate(flops=9 * 10**9, bytes_accessed=5 * 10**6, transcendentals=2 * 10**6),
    )(
        volume.reshape(cells, channels),
        plane_weight.reshape(layers * TAPS * TAPS * group, channels),
        norm_gain,
        expand_weight.reshape(layers * channels, hid),
        down_weight.reshape(layers * hid, channels),
        depth_weight.transpose(1, 0, 2),
    )
    return out.reshape(volume.shape)


def solution(mesh):
    placed = (P(("parts", "slab"), None, None, None), P(), P(), P(), P(), P())
    return jax.shard_map(
        functools.partial(shards, mesh.shape["slab"]),
        mesh=mesh,
        in_specs=placed,
        out_specs=P(("parts", "slab"), None, None, None),
        check_vma=False,
    )
```

time: 32.4 us -> 32.9 us (1.015)
  Pallas kernels: 30.3 us -> 30.8 us
    pallas_call x1, Pallas kernels: 30.3 us -> 30.8 us  [shards(): pl.pallas_call(functools.partial(kernel, devices, extent_x, extent_y), ou...]
where the time goes in v3:
time: 32.9 us; the launch traced here: 32.7 us
  Pallas kernels  30.8 us (94%)
  local copies, waits for them, and re-layouts  1.88 us (6%)
    pallas_call x1, Pallas kernels, shards(): pl.pallas_call(functools.partial(kernel, devices, extent_x, extent_y), ou...  30.8 us
    unnamed x1, local copies, waits for them, and re-layouts  1.88 us

profile of v3, /device:TPU:1, one launch (start us, length us, event | category | flops | bytes accessed | tf_op | source)
XLA Modules:
  0.0 32.7 jit_solution(1982839963116417065)
XLA Ops:
  0.0 30.8 %shard_map.64 = bf16[1024,256]{1,0:T(8,128)(2,1)} custom-call(bf16[1024,256]{1,0:T(8,128)(2,1)} %bitcast.9, bf16[800,256]{1,0:T(8,128)(2,1)} %bitcast.10, bf16[2,256]{1,0:T(2,128)(2,1)} %gain_ref.1, bf16[512,1024]{1,0:T(8,128)(2,1)} %bitcast.7, bf16[2048,256]{1,0:T(8,128)(2,1)} %bitcast.8, bf16[3,2,256]{2,1,0:T(2,128)(2,1)} %bitcast.11), custom_call_target="tpu_custom_call" | custom-call | flops 8999999488 | bytes 5000000 | tf_op jit(solution)/shard_map/pallas_call | solution.py:297
  30.8 1.9 %copy.8 = bf16[1,16,64,256]{3,2,1,0:T(8,128)(2,1)} copy(bf16[1,16,64,256]{3,2,1,0:T(8,128)(2,1)} %bitcast.6) | data formatting | bytes 1048576

commit v4 on v3

--- a/solution.py
+++ b/solution.py
@@ -10,7 +10,7 @@
 DILATIONS = (1, 4)
 TAPS = 5
 EPSILON = 1e-06
-CHUNK_X = 4
+CHUNK_X = 2
 PACK = 4
 CONV_CHUNKS = 2
 
@@ -135,7 +135,7 @@
             total = None
             for dx in range(TAPS):
                 part = jnp.dot(
-                    window[at + dx * blocks:at + dx * blocks + size, q * depth:(q + 1) * depth],
+                    window[pl.ds(pl.multiple_of(at + dx * blocks, blocks), size), q * depth:(q + 1) * depth],
                     taps[(dx * PACK + q) * depth:(dx * PACK + q + 1) * depth, :],
                     preferred_element_type=f32)
                 total = part if total is None else total + part
@@ -161,8 +161,8 @@
                 for j, value in ((2 * v, jnp.where(low, a, swap(b))), (2 * v + 1, jnp.where(low, swap(a), b))):
                     value = value.astype(bf16)
                     for c in range(count):
-                        to = (first_chunk + c) * rows + j * plane_rows
-                        normed[to:to + plane_rows, h * half:(h + 1) * half] = (
+                        to = pl.multiple_of((first_chunk + c) * rows + j * plane_rows, plane_rows)
+                        normed[pl.ds(to, plane_rows), h * half:(h + 1) * half] = (
                             value[c * plane_rows:(c + 1) * plane_rows])
 
     def mix(layer, chunk):
@@ -250,13 +250,15 @@
         fill(i, [value[j * plane_rows:(j + 1) * plane_rows] for j in range(PACK)])
         return carry
 
-    filled = 0
-    for start in range(0, chunks, CONV_CHUNKS):
-        need = min(start + CONV_CHUNKS + 1, chunks)
-        lax.fori_loop(filled, need, refill, 0)
-        filled = need
+    lax.fori_loop(0, 1, refill, 0)
+
+    def step(k, carry):
+        start = k * CONV_CHUNKS
+        lax.fori_loop(start + 1, jnp.minimum(start + 1 + CONV_CHUNKS, chunks), refill, 0)
         conv(1, start, CONV_CHUNKS)
         mix_and_send(1, start, CONV_CHUNKS)
+        return carry
+    lax.fori_loop(0, chunks // CONV_CHUNKS, step, 0)
 
     def store(i):
         at = pl.multiple_of(i * rows, rows)

time: 32.9 us -> 33.5 us (1.018)
  Pallas kernels: 30.8 us -> 31.4 us
    pallas_call x1, Pallas kernels: 30.8 us -> 31.4 us  [shards(): pl.pallas_call(functools.partial(kernel, devices, extent_x, extent_y), ou...]
where the time goes in v4:
time: 33.5 us; the launch traced here: 33.2 us
  Pallas kernels  31.4 us (94%)
  local copies, waits for them, and re-layouts  1.88 us (6%)
    pallas_call x1, Pallas kernels, shards(): pl.pallas_call(functools.partial(kernel, devices, extent_x, extent_y), ou...  31.4 us
    unnamed x1, local copies, waits for them, and re-layouts  1.88 us

profile of v4, /device:TPU:1, one launch (start us, length us, event | category | flops | bytes accessed | tf_op | source)
XLA Modules:
  0.0 33.2 jit_solution(16064875767179013061)
XLA Ops:
  0.0 31.4 %shard_map.64 = bf16[1024,256]{1,0:T(8,128)(2,1)} custom-call(bf16[1024,256]{1,0:T(8,128)(2,1)} %bitcast.9, bf16[800,256]{1,0:T(8,128)(2,1)} %bitcast.10, bf16[2,256]{1,0:T(2,128)(2,1)} %gain_ref.1, bf16[512,1024]{1,0:T(8,128)(2,1)} %bitcast.7, bf16[2048,256]{1,0:T(8,128)(2,1)} %bitcast.8, bf16[3,2,256]{2,1,0:T(2,128)(2,1)} %bitcast.11), custom_call_target="tpu_custom_call" | custom-call | flops 8999999488 | bytes 5000000 | tf_op jit(solution)/shard_map/pallas_call | solution.py:299
  31.4 1.9 %copy.8 = bf16[1,16,64,256]{3,2,1,0:T(8,128)(2,1)} copy(bf16[1,16,64,256]{3,2,1,0:T(8,128)(2,1)} %bitcast.6) | data formatting | bytes 1048576

commit v5 on v4

--- a/solution.py
+++ b/solution.py
@@ -231,14 +231,17 @@
             cur[pl.ds(at + j * plane_rows, plane_rows), :] = planes[j].astype(bf16)
         fill(i, planes)
         return carry
-    lax.fori_loop(0, chunks, first_fill, 0)
+    lax.fori_loop(0, CONV_CHUNKS + 1, first_fill, 0)
     loads[0].wait()
     build_taps(0)
-    conv(0, 0, chunks)
+    conv(0, 0, CONV_CHUNKS)
     loads[2].wait()
     loads[3].wait()
     pl.semaphore_wait(barrier, sum(inside(other).astype(jnp.int32) for _, _, other in reach))
-    mix_and_send(0, 0, chunks)
+    mix_and_send(0, 0, CONV_CHUNKS)
+    lax.fori_loop(CONV_CHUNKS + 1, chunks, first_fill, 0)
+    conv(0, CONV_CHUNKS, chunks - CONV_CHUNKS)
+    mix_and_send(0, CONV_CHUNKS, chunks - CONV_CHUNKS)
 
     build_taps(1)
 
@@ -300,7 +303,7 @@
         functools.partial(kernel, devices, extent_x, extent_y),
         out_shape=jax.ShapeDtypeStruct((cells, channels), bf16),
         in_specs=[far, far, whole, far, far, whole],
-        out_specs=far,
+        out_specs=pl.BlockSpec(memory_space=pl.ANY),
         scratch_shapes=[
             pltpu.VMEM((cells, channels), bf16),
             pltpu.VMEM((2, cells, channels // 2), jnp.float32),
@@ -321,7 +324,7 @@
             pltpu.SemaphoreType.DMA((chunks,)),
         ],
         compiler_params=pltpu.CompilerParams(
-            collective_id=0, has_side_effects=True, vmem_limit_bytes=63 * 1024 * 1024),
+            collective_id=0, has_side_effects=True, vmem_limit_bytes=54 * 1024 * 1024),
         cost_estimate=pl.CostEstimate(flops=9 * 10**9, bytes_accessed=5 * 10**6, transcendentals=2 * 10**6),
     )(
         volume.reshape(cells, channels),

time: 33.5 us -> 33 us (0.985)
  Pallas kernels: 31.4 us -> 30.9 us
    pallas_call x1, Pallas kernels: 31.4 us -> 30.9 us  [shards(): pl.pallas_call(functools.partial(kernel, devices, extent_x, extent_y), ou...]
where the time goes in v5:
time: 33 us; the launch traced here: 32.7 us
  Pallas kernels  30.9 us (94%)
  local copies, waits for them, and re-layouts  1.88 us (6%)
    pallas_call x1, Pallas kernels, shards(): pl.pallas_call(functools.partial(kernel, devices, extent_x, extent_y), ou...  30.9 us
    unnamed x1, local copies, waits for them, and re-layouts  1.88 us

profile of v5, /device:TPU:1, one launch (start us, length us, event | category | flops | bytes accessed | tf_op | source)
XLA Modules:
  0.0 32.7 jit_solution(4823659665814036943)
XLA Ops:
  0.0 30.9 %shard_map.64 = bf16[1024,256]{1,0:T(8,128)(2,1)} custom-call(bf16[1024,256]{1,0:T(8,128)(2,1)} %bitcast.9, bf16[800,256]{1,0:T(8,128)(2,1)} %bitcast.10, bf16[2,256]{1,0:T(2,128)(2,1)} %gain_ref.1, bf16[512,1024]{1,0:T(8,128)(2,1)} %bitcast.7, bf16[2048,256]{1,0:T(8,128)(2,1)} %bitcast.8, bf16[3,2,256]{2,1,0:T(2,128)(2,1)} %bitcast.11), custom_call_target="tpu_custom_call" | custom-call | flops 8999999488 | bytes 5000000 | tf_op jit(solution)/shard_map/pallas_call | solution.py:302
  30.9 1.9 %copy.8 = bf16[1,16,64,256]{3,2,1,0:T(8,128)(2,1)} copy(bf16[1,16,64,256]{3,2,1,0:T(8,128)(2,1)} %bitcast.6) | data formatting | bytes 1048576

commit v6 on v5

--- a/solution.py
+++ b/solution.py
@@ -10,9 +10,9 @@
 DILATIONS = (1, 4)
 TAPS = 5
 EPSILON = 1e-06
-CHUNK_X = 2
+CHUNK_X = 4
 PACK = 4
-CONV_CHUNKS = 2
+CONV_CHUNKS = 1
 
 
 def kernel(devices, extent_x, extent_y, vol_hbm, plane_hbm, gain_ref, expand_hbm, down_hbm, depth_ref, out_hbm,
@@ -231,7 +231,7 @@
             cur[pl.ds(at + j * plane_rows, plane_rows), :] = planes[j].astype(bf16)
         fill(i, planes)
         return carry
-    lax.fori_loop(0, CONV_CHUNKS + 1, first_fill, 0)
+    lax.fori_loop(0, CONV_CHUNKS + 1, first_fill, 0, unroll=True)
     loads[0].wait()
     build_taps(0)
     conv(0, 0, CONV_CHUNKS)
@@ -239,7 +239,7 @@
     loads[3].wait()
     pl.semaphore_wait(barrier, sum(inside(other).astype(jnp.int32) for _, _, other in reach))
     mix_and_send(0, 0, CONV_CHUNKS)
-    lax.fori_loop(CONV_CHUNKS + 1, chunks, first_fill, 0)
+    lax.fori_loop(CONV_CHUNKS + 1, chunks, first_fill, 0, unroll=True)
     conv(0, CONV_CHUNKS, chunks - CONV_CHUNKS)
     mix_and_send(0, CONV_CHUNKS, chunks - CONV_CHUNKS)
 

time: 33 us -> 32.7 us (level)
  no operation moved by 1% of the time
where the time goes in v6:
time: 32.7 us; the launch traced here: 32.5 us
  Pallas kernels  30.6 us (94%)
  local copies, waits for them, and re-layouts  1.88 us (6%)
    pallas_call x1, Pallas kernels, shards(): pl.pallas_call(functools.partial(kernel, devices, extent_x, extent_y), ou...  30.6 us
    unnamed x1, local copies, waits for them, and re-layouts  1.88 us

profile of v6, /device:TPU:1, one launch (start us, length us, event | category | flops | bytes accessed | tf_op | source)
XLA Modules:
  0.0 32.5 jit_solution(11240506643282406237)
XLA Ops:
  0.0 30.6 %shard_map.64 = bf16[1024,256]{1,0:T(8,128)(2,1)} custom-call(bf16[1024,256]{1,0:T(8,128)(2,1)} %bitcast.9, bf16[800,256]{1,0:T(8,128)(2,1)} %bitcast.10, bf16[2,256]{1,0:T(2,128)(2,1)} %gain_ref.1, bf16[512,1024]{1,0:T(8,128)(2,1)} %bitcast.7, bf16[2048,256]{1,0:T(8,128)(2,1)} %bitcast.8, bf16[3,2,256]{2,1,0:T(2,128)(2,1)} %bitcast.11), custom_call_target="tpu_custom_call" | custom-call | flops 8999999488 | bytes 5000000 | tf_op jit(solution)/shard_map/pallas_call | solution.py:302
  30.6 1.9 %copy.8 = bf16[1,16,64,256]{3,2,1,0:T(8,128)(2,1)} copy(bf16[1,16,64,256]{3,2,1,0:T(8,128)(2,1)} %bitcast.6) | data formatting | bytes 1048576

commit v7 on v2

--- a/solution.py
+++ b/solution.py
@@ -13,7 +13,7 @@
 CHUNK_X = 4
 
 
-def kernel(devices, extent_x, extent_y, vol_hbm, plane_hbm, gain_ref, expand_hbm, down_hbm, depth_ref, out_hbm,
+def kernel(devices, extent_x, extent_y, vol_hbm, plane_hbm, gain_ref, expand_hbm, down_hbm, depth_ref, base_hbm, term_hbm,
            cur, plane, expand, down, mask, taps, window, mixed, lower, upper, result,
            load_sem, send_sem, recv_sem, out_sem):
     me = lax.axis_index("slab")
@@ -129,8 +129,7 @@
         term = (coeffs[0] * lower[layer, here, :].astype(jnp.float32)
                 + coeffs[1] * mixed[layer, here, :].astype(jnp.float32)
                 + coeffs[2] * upper[layer, here, :].astype(jnp.float32))
-        term = term.astype(jnp.bfloat16).astype(jnp.float32)
-        return (cur[here, :].astype(jnp.float32) + term).astype(jnp.bfloat16)
+        return term.astype(jnp.bfloat16)
 
     loads[0].wait()
     build_taps(0)
@@ -158,7 +157,7 @@
         def _():
             receive(0, i)
             at = pl.multiple_of(i * rows, rows)
-            value = combine(0, at)
+            value = (cur[pl.ds(at, rows), :].astype(jnp.float32) + combine(0, at).astype(jnp.float32)).astype(jnp.bfloat16)
             cur[pl.ds(at, rows), :] = value
             fill(at, value.astype(jnp.float32))
 
@@ -171,7 +170,10 @@
 
     def store(i):
         at = pl.multiple_of(i * rows, rows)
-        return pltpu.make_async_copy(result.at[pl.ds(at, rows), :], out_hbm.at[pl.ds(at, rows), :], out_sem.at[i])
+        return pltpu.make_async_copy(result.at[pl.ds(at, rows), :], term_hbm.at[pl.ds(at, rows), :], out_sem.at[i])
+
+    base = pltpu.make_async_copy(cur, base_hbm, load_sem.at[0])
+    base.start()
 
     def last(i, carry):
         receive(1, i)
@@ -189,6 +191,7 @@
                 copy(layer, side, i).wait_send()
         return carry
     lax.fori_loop(0, chunks, drain, 0)
+    base.wait()
 
 
 def shards(devices, volume, plane_weight, norm_gain, expand_weight, down_weight, depth_weight):
@@ -200,11 +203,11 @@
     bf16 = jnp.bfloat16
     whole = pl.BlockSpec(memory_space=pltpu.VMEM)
     far = pl.BlockSpec(memory_space=pl.ANY)
-    out = pl.pallas_call(
+    base, term = pl.pallas_call(
         functools.partial(kernel, devices, extent_x, extent_y),
-        out_shape=jax.ShapeDtypeStruct((cells, channels), bf16),
+        out_shape=[jax.ShapeDtypeStruct((cells, channels), bf16)] * 2,
         in_specs=[far, far, whole, far, far, whole],
-        out_specs=far,
+        out_specs=[far, far],
         scratch_shapes=[
             pltpu.VMEM((cells, channels), bf16),
             pltpu.VMEM((layers * TAPS * TAPS * group, channels), bf16),
@@ -223,7 +226,7 @@
             pltpu.SemaphoreType.DMA((chunks,)),
         ],
         compiler_params=pltpu.CompilerParams(
-            collective_id=0, has_side_effects=True, vmem_limit_bytes=63 * 1024 * 1024),
+            collective_id=0, has_side_effects=True, vmem_limit_bytes=54 * 1024 * 1024),
         cost_estimate=pl.CostEstimate(flops=9 * 10**9, bytes_accessed=5 * 10**6, transcendentals=2 * 10**6),
     )(
         volume.reshape(cells, channels),
@@ -233,7 +236,7 @@
         down_weight.reshape(layers * hid, channels),
         depth_weight.transpose(1, 0, 2),
     )
-    return out.reshape(volume.shape)
+    return (base.astype(jnp.float32) + term.astype(jnp.float32)).astype(bf16).reshape(volume.shape)
 
 
 def solution(mesh):

time: 32.4 us -> 32.6 us (level)
  other arithmetic: 0 us -> 2.12 us
  local copies, waits for them, and re-layouts: 1.88 us -> 0 us
    convert_element_type x0 -> x1, other arithmetic: none -> 2.12 us  [shards(): (base.astype(jnp.float32) + term.astype(jnp.float32)).astype(bf16)]
    unnamed x1 -> x0, local copies, waits for them, and re-layouts: 1.88 us -> none
where the time goes in v7:
time: 32.6 us; the launch traced here: 32.4 us
  Pallas kernels  30.3 us (93%)
  other arithmetic  2.12 us (7%)
    pallas_call x1, Pallas kernels, shards(): pl.pallas_call(functools.partial(kernel, devices, extent_x, extent_y), ou...  30.3 us
    convert_element_type x1, other arithmetic, shards(): (base.astype(jnp.float32) + term.astype(jnp.float32)).astype(bf16)  2.12 us

profile of v7, /device:TPU:1, one launch (start us, length us, event | category | flops | bytes accessed | tf_op | source)
XLA Modules:
  0.0 32.4 jit_solution(11241104354672773782)
XLA Ops:
  0.0 30.3 %shard_map.64 = (bf16[1024,256]{1,0:T(8,128)(2,1)}, bf16[1024,256]{1,0:T(8,128)(2,1)}) custom-call(bf16[1024,256]{1,0:T(8,128)(2,1)} %bitcast.8, bf16[800,256]{1,0:T(8,128)(2,1)} %bitcast.9, bf16[2,256]{1,0:T(2,128)(2,1)} %gain_ref.1, bf16[512,1024]{1,0:T(8,128)(2,1)} %bitcast.6, bf16[2048,256]{1,0:T(8,128)(2,1)} %bitcast.7, bf16[3,2,256]{2,1,0:T(2,128)(2,1)} %bitcast.10), custom_call_target="tpu_custom_call" | custom-call | flops 8999999488 | bytes 5000000 | tf_op jit(solution)/shard_map/pallas_call | solution.py:206
  30.3 2.1 %add_convert_fusion = bf16[1024,256]{1,0:T(8,128)(2,1)} fusion(bf16[1024,256]{1,0:T(8,128)(2,1)} %get-tuple-element.8, bf16[1024,256]{1,0:T(8,128)(2,1)} %get-tuple-element.7), kind=kLoop, calls=%fused_computation | loop fusion | flops 1048576 | bytes 1572864 | tf_op jit(solution)/shard_map/convert_element_type | solution.py:239
